TPU v7x, 256 devices: a whole 4x4x8 slice. The times are simulated.
256 devices in a mesh: ia: 16 (over z, y_lo), ja: 16 (over y_hi, x, core).
Axes of the slice: x: 4, y: 4 (y_hi: 2, y_lo: 2; y = y_hi * 2 + y_lo), z: 8, core: 2. Of those that a mesh axis runs over, the one named last changes fastest.
Arguments:
- amplitudes: float32 [64, 64, 384, 384], P('ia', 'ja'), may hold values from -6 to 6
- integrals: float32 [768, 384, 384], P('ia', 'ja'), may hold values from -0.0625 to 0.0625
- occ_irrep: int32 [64], replicated, may hold values from 0 to 7
- vir_irrep: int32 [6], replicated, may hold values from 0 to 7
- occ_energy: float32 [64], replicated, may hold values from -2 to -0.3
- vir_energy: float32 [384], replicated, may hold values from 0.2 to 2.5
Outputs:
- residual: float32 [64, 64, 768], P('ia', None, 'ja')
All inputs are finite; a program needn't handle non-finite values.
Results may differ from a plain program's by a relative error of at most 0.0003.
Values sent between devices are 32-bit elements; how exact they have to be, the bound alone decides.
No kernel may reach another device: no remote copies, remote signals or barrier semaphores. Data moves between devices by JAX's collectives and lax.ppermute only.
A program may use at most 192 MiB of HBM per device.

v0:
```python
import jax
import jax.numpy as jnp
from jax import lax
from jax.sharding import PartitionSpec as P

O = 64
NV = 384
VT = 64
SA = 2


def tile_labels(vir_irrep):
    return jnp.broadcast_to(vir_irrep[:, None], (NV // VT, VT)).reshape(NV)


def masked_rows(values, labels, pair_cd):
    return jnp.where(labels[:, None, None] == pair_cd[None], values, 0.0)


def contract_rows(left_rows, right_rows):
    return lax.dot_general(
        left_rows,
        right_rows,
        (((1,), (1,)), ((), ())),
        precision=lax.Precision.HIGHEST,
        preferred_element_type=jnp.float32,
    )


def local(amplitudes, integrals, occ_irrep, vir_irrep, occ_energy, vir_energy):
    count_ia = lax.axis_size("ia")
    count_ja = lax.axis_size("ja")
    index_ia = lax.axis_index("ia")
    index_ja = lax.axis_index("ja")
    i_local = O // count_ia
    c_local = NV // count_ja
    orbital = tile_labels(vir_irrep)
    pair_ab = jnp.bitwise_xor(orbital[:SA, None], orbital[None, :]).reshape(SA * NV)
    ab_energy = (vir_energy[:SA, None] + vir_energy[None, :]).reshape(SA * NV)
    c_labels = lax.dynamic_slice_in_dim(orbital, index_ja * c_local, c_local)
    own_occ = lax.dynamic_slice_in_dim(occ_irrep, index_ia * i_local, i_local)
    exchanged = lax.all_to_all(amplitudes, "ja", split_axis=2, concat_axis=1, tiled=True)
    pair_cd = jnp.bitwise_xor(c_labels[:, None], orbital[None, :])
    pair_ij = jnp.bitwise_xor(own_occ[:, None], occ_irrep[None, :])
    kept_rows = jnp.where(pair_ij[:, :, None, None] == pair_cd[None, None], exchanged, 0.0).reshape(
        i_local * O, c_local * NV
    )
    portion = lax.all_gather(integrals, "ia", axis=0, tiled=True)
    integral_block = masked_rows(portion, pair_ab, pair_cd).reshape(portion.shape[0], c_local * NV)
    partial_value = contract_rows(kept_rows, integral_block).reshape(i_local, O, SA * NV)
    ladder = lax.psum_scatter(partial_value, "ja", scatter_dimension=2, tiled=True)
    mirror = lax.all_to_all(ladder, "ia", split_axis=1, concat_axis=0, tiled=True)
    difference = ladder - jnp.transpose(mirror, (1, 0, 2))
    slab_local = difference.shape[2]
    ab_part = lax.dynamic_slice_in_dim(ab_energy, index_ja * slab_local, slab_local)
    occ_part = lax.dynamic_slice_in_dim(occ_energy, index_ia * i_local, i_local)
    denominator = occ_part[:, None, None] + occ_energy[None, :, None] - ab_part[None, None, :]
    return difference / denominator


def solution(mesh):
    in_specs = (P("ia", "ja", None, None), P("ia", "ja", None), P(), P(), P(), P())
    out_specs = P("ia", None, "ja")
    return jax.shard_map(local, mesh=mesh, in_specs=in_specs, out_specs=out_specs, check_vma=False)
```

profile of v0, /device:TPU:1, one launch (start us, length us, event | category | flops | bytes accessed | tf_op | source)
XLA Modules:
  0.0 898.6 jit_solution(7914075540107749748)
XLA Ops:
  6.5 0.7 all-gather.2.cloned.1.call-update
  7.3 13.4 %copy.15 = f32[4,4,384,384]{3,1,0,2:T(4,128)} copy(f32[4,4,384,384]{3,2,1,0:T(8,128)} %param.6) | data formatting | bytes 18874368 | tf_op args[0]
  20.6 8.6 all-to-all-start
  29.2 0.2 reduce-scatter.2.cloned.1.call-start
  29.4 0.1 xor.61
  29.5 0.1 dynamic_slice.12
  29.7 0.1 reshape.173
  29.7 0.1 dynamic_slice.13
  29.9 0.1 broadcast_xor_fusion
  30.0 0.1 broadcast_xor_fusion.1
  30.1 168.0 %all-to-all-done = f32[4,4,384,384]{3,1,0,2:T(4,128)} async-done(((f32[4,4,384,384]{3,1,0,2:T(4,128)}), f32[4,4,384,384]{3,1,0,2:T(4,128)}, u32[]{:S(2)}, u32[]{:S(2)}) %all-to-all-start) | async-done | bytes 9437216 | tf_op jit(solution)/shard_map/all_to_all | solution.py:42
  198.0 10.0 %compare_select_fusion.1 = f32[4,16,4,24,384]{4,2,0,3,1:T(4,128)} fusion(f32[4,16,4,24,384]{4,2,0,3,1:T(4,128)} %bitcast.1, s32[24,384]{1,0:T(8,128)S(1)} %broadcast_xor_fusion, s32[4,16,4]{2,0,1:T(4,128)S(1)} %broadcast_xor_fusion.1), kind=kLoop, calls=%fused_computation.1 | loop fusion | flops 4718592 | bytes 18912256 | tf_op jit(solution)/shard_map/jit(_where)/select_n | solution.py:45
  208.0 10.4 %copy.16 = f32[4,16,4,24,384]{4,3,2,1,0:T(8,128)} copy(f32[4,16,4,24,384]{4,2,0,3,1:T(4,128)} %compare_select_fusion.1) | data formatting | bytes 18874368 | tf_op jit(solution)/shard_map/jit(_where)/select_n | solution.py:45
  218.4 9.9 %select_n.26 = f32[4,64,9216]{2,1,0:T(8,128)} reshape(f32[4,16,4,24,384]{4,3,2,1,0:T(8,128)} %copy.16) | data formatting | bytes 18874368 | tf_op jit(solution)/shard_map/jit(_where)/select_n | solution.py:45
  228.3 468.5 %all-gather.2.cloned.1.call-done = f32[768,24,384]{2,1,0:T(8,128)} async-done(((f32[48,24,384]{2,1,0:T(8,128)}), f32[768,24,384]{2,1,0:T(8,128)}) %all-gather.2.cloned.1.call-update) | async-done | bytes 28311568 | tf_op jit(solution)/shard_map/all_gather | solution.py:48
  696.8 21.4 %compare_select_fusion = f32[768,24,384]{2,1,0:T(8,128)} fusion(f32[768,24,384]{2,1,0:T(8,128)} %all-gather.2.cloned.1.call-done, s32[24,384]{1,0:T(8,128)S(1)} %broadcast_xor_fusion, s32[768]{0:T(1024)S(1)} %xor.70), kind=kLoop, calls=%fused_computation | loop fusion | flops 14155776 | bytes 56663040 | tf_op jit(solution)/shard_map/jit(_where)/select_n | solution.py:17
  718.3 28.6 %reshape.175 = f32[768,9216,1]{1,0,2:T(8,128)} reshape(f32[768,24,384]{2,1,0:T(8,128)} %compare_select_fusion) | data formatting | bytes 56623104 | tf_op jit(solution)/shard_map/reshape | solution.py:49
  746.9 49.1 %fusion.1 = f32[4,64,768]{1,2,0:T(8,128)} fusion(f32[4,64,9216]{2,1,0:T(8,128)} %select_n.26, f32[768,9216,1]{1,0,2:T(8,128)} %reshape.175), kind=kOutput, calls=%fused_computation.9 | convolution fusion | flops 21743271936 | bytes 38535168 | tf_op jit(solution)/shard_map/dot_general | solution.py:21
  796.0 0.1 dynamic_slice.14
  796.2 75.5 %reduce-scatter.2.cloned.1.call-done = f32[4,64,48]{1,2,0:T(8,128)} async-done(((f32[4,64,768]{1,2,0:T(8,128)}), f32[4,64,48]{1,2,0:T(8,128)}) %reduce-scatter.2.cloned.1.call-update) | async-done | bytes 49168 | tf_op jit(solution)/shard_map/reduce_scatter | solution.py:51
  871.7 1.0 copy.17
  872.7 0.8 reshape.177
  873.5 7.3 all-to-all-start.1
  880.8 0.1 broadcast_add_fusion.1
  880.9 0.1 dynamic_slice.15
  880.9 7.6 all-to-all-done.1
  888.5 0.5 broadcast.108
  889.0 0.8 reduce
  889.8 0.2 reshape.178
  890.0 0.1 copy.19
  890.1 0.1 copy.20
  890.2 1.6 fusion
  (19 shorter events, 0.3 us)
Async XLA Ops:
  6.5 690.3 %all-gather.2.cloned.1.call-start = ((), (), s32[]{:S(2)}) async-start(), calls=%async_computation.3 | async-start | bytes 30081024 | tf_op jit(solution)/shard_map/all_gather | solution.py:48
  20.6 8.8 copy-start.1
  20.6 9.0 copy-start.2
  20.6 177.4 %all-to-all-start = ((f32[4,4,384,384]{3,1,0,2:T(4,128)}), f32[4,4,384,384]{3,1,0,2:T(4,128)}, u32[]{:S(2)}, u32[]{:S(2)}) async-start(f32[4,4,384,384]{3,1,0,2:T(4,128)} %copy.15), calls=%async_computation | async-start | bytes 18874368 | tf_op jit(solution)/shard_map/all_to_all | solution.py:42
  29.2 842.5 %reduce-scatter.2.cloned.1.call-start = ((), (), s32[]{:S(2)}) async-start(), calls=%async_computation.4 | async-start | bytes 1671168 | tf_op jit(solution)/shard_map/reduce_scatter | solution.py:51
  746.9 49.1 %copy-start.3 = (f32[64]{0:T(128)S(1)}, f32[64]{0:T(128)}, u32[]{:S(2)}) copy-start(f32[64]{0:T(128)} %param.10) | copy-start | bytes 772
  746.9 49.2 %copy-start = (f32[384]{0:T(512)S(1)}, f32[384]{0:T(512)}, u32[]{:S(2)}) copy-start(f32[384]{0:T(512)} %param.11) | copy-start | bytes 4612
  746.9 49.2 %slice-start = ((f32[384]{0:T(512)}), f32[2]{0:T(128)S(1)}, s32[]{:S(2)}) async-start(f32[384]{0:T(512)} %param.11), calls=%async_computation.5 | async-start | bytes 1024 | tf_op jit(solution)/shard_map/slice | solution.py:39
  873.5 15.1 %all-to-all-start.1 = ((f32[16,1,768]{2,1,0:T(1,128)}), f32[16,1,768]{2,1,0:T(1,128)S(1)}, u32[]{:S(2)}, u32[]{:S(2)}) async-start(f32[16,1,768]{2,1,0:T(1,128)} %reshape.177), calls=%async_computation.2 | async-start | bytes 98304 | tf_op jit(solution)/shard_map/all_to_all | solution.py:52
Sparse Core Ops, SparseCore 0:
  9.1 687.6 all-gather.1
  796.1 75.5 reduce-scatter.1
where the time goes:
time: 902 us; the launch traced here: 899 us
  waiting for transfers between devices  720 us (80%)
  local copies, waits for them, and re-layouts  65.5 us (7%)
  matrix products  49.1 us (5%)
  other arithmetic  34.2 us (4%)
  starting transfers between devices  16.1 us (2%)
  between operations  13.5 us (1%)
    all_gather x1, waiting for transfers between devices, local(): portion = lax.all_gather(integrals, 'ia', axis=0, tiled=True)  468 us
    all_to_all x1, waiting for transfers between devices, local(): lax.all_to_all(amplitudes, 'ja', split_axis=2, concat_axis=1, tiled=True)  168 us
    reduce_scatter x1, waiting for transfers between devices, local(): lax.psum_scatter(partial_value, 'ja', scatter_dimension=2, tiled=True)  75.5 us
    dot_general x1, matrix products, contract_rows(): lax.dot_general(left_rows, right_rows, (((1,), (1,)), ((), ())), precisio...  49.1 us
    reshape x1, local copies, waits for them, and re-layouts, local(): masked_rows(portion, pair_ab, pair_cd)  28.6 us
    select_n x1, other arithmetic, masked_rows(): return jnp.where(labels[:, None, None] == pair_cd[None], values, 0.0)  21.4 us
    select_n x2, local copies, waits for them, and re-layouts, local(): jnp.where(pair_ij[:, :, None, None] == pair_cd[None, None], exchanged, 0.0)  20.3 us
  transfers between devices with their start and end apart: 4, of which 4 were waited for; matrix products, arithmetic and copies ran while one was open for 5% of the time, Pallas kernels for 0%

commit v1 on v0

v1 whole, which is shorter than its diff:
```python
import functools

import jax
import jax.numpy as jnp
from jax import lax
from jax.experimental import pallas as pl
from jax.experimental.pallas import tpu as pltpu
from jax.sharding import Mesh, PartitionSpec as P

O = 64
NV = 384
VT = 64
SA = 2
NVT = NV // VT
Z = 8
YL = 2
JA = 16
NI = 4
PAIRS = NI * NI
CB = NV // JA
CK = CB // YL
AB = SA * NV // (Z * YL)
ROWS = JA * PAIRS
LANES = 128
VMEM_LIMIT = 60 * 1024 * 1024


def slot_tiles(wanted, vir, tile):
    lane = lax.broadcasted_iota(jnp.int32, wanted.shape, wanted.ndim - 1)
    slot = jnp.where(lane < VT, 2 * tile, 2 * tile + 1)
    count = jnp.zeros(wanted.shape, jnp.int32)
    chosen = jnp.full(wanted.shape, -1, jnp.int32)
    for td in range(NVT):
        match = wanted == vir[td]
        chosen = jnp.where(match & (count == slot), td, chosen)
        count = jnp.where(match, count + 1, count)
    return chosen


def pack_tiles(block, chosen_of):
    lane = lax.broadcasted_iota(jnp.int32, block.shape[:2] + (LANES,), 2)
    low = lane < VT
    packed = [jnp.zeros(block.shape[:2] + (LANES,), jnp.float32) for _ in chosen_of]
    for k in range(NV // LANES):
        part = block[:, :, k * LANES : (k + 1) * LANES]
        turned = pltpu.roll(part, VT, 2)
        even = jnp.where(low, part, turned)
        odd = jnp.where(low, turned, part)
        for t, chosen in enumerate(chosen_of):
            packed[t] = jnp.where(chosen == 2 * k, even, packed[t])
            packed[t] = jnp.where(chosen == 2 * k + 1, odd, packed[t])
    return packed


def pack_amplitudes_kernel(tiles, occ, vir, t_ref, out_ref, chosen_ref):
    step = pl.program_id(0)

    @pl.when(step == 0)
    def _():
        first_i = NI * (YL * lax.axis_index("z") + lax.axis_index("yl"))
        first_j = NI * lax.axis_index("ja")
        for p in range(PAIRS):
            label = occ[first_i + p // NI] ^ occ[first_j + p % NI]
            for tc in range(NVT):
                wanted = jnp.full((8, LANES), label ^ vir[tc], jnp.int32)
                for t in range(tiles):
                    chosen_ref[tc, t, p] = slot_tiles(wanted, vir, t)

    for b in range(CB // 8):
        tc = (step * (CB // 8) + b) // (VT // 8)
        block = t_ref[:, b * 8 : (b + 1) * 8, :]
        packed = pack_tiles(block, [chosen_ref[tc, t] for t in range(tiles)])
        for t in range(tiles):
            turned = jnp.swapaxes(packed[t], 0, 1)
            for r in range(8):
                c = b * 8 + r
                out_ref[c // CK, 0, c % CK, :, t * LANES : (t + 1) * LANES] = turned[r]


def pack_amplitudes(amplitudes, occ_irrep, vir_irrep, tiles):
    width = tiles * LANES
    return pl.pallas_call(
        functools.partial(pack_amplitudes_kernel, tiles),
        out_shape=jax.ShapeDtypeStruct((YL, JA, CK, PAIRS, width), jnp.float32),
        grid=(JA,),
        in_specs=[
            pl.BlockSpec(memory_space=pltpu.SMEM),
            pl.BlockSpec(memory_space=pltpu.SMEM),
            pl.BlockSpec((PAIRS, CB, NV), lambda s: (0, s, 0)),
        ],
        out_specs=pl.BlockSpec((YL, 1, CK, PAIRS, width), lambda s: (0, s, 0, 0, 0)),
        scratch_shapes=[pltpu.VMEM((NVT, tiles, PAIRS, 8, LANES), jnp.int32)],
        compiler_params=pltpu.CompilerParams(vmem_limit_bytes=VMEM_LIMIT),
        cost_estimate=pl.CostEstimate(flops=10**7, bytes_accessed=14 * 10**6, transcendentals=0),
    )(occ_irrep, vir_irrep, amplitudes.reshape(PAIRS, NV, NV))


def pack_integrals_kernel(tiles, vir, v_ref, out_ref):
    step = pl.program_id(0)
    ia = YL * lax.axis_index("z") + lax.axis_index("yl")
    tb = (AB * (ia % (Z * YL // SA)) + 16 * step) // VT
    for b in range(CB // 8):
        tc = (lax.axis_index("ja") * (CB // 8) + b) // (VT // 8)
        wanted = jnp.full((1, 8, LANES), vir[0] ^ vir[tb] ^ vir[tc], jnp.int32)
        packed = pack_tiles(v_ref[:, b * 8 : (b + 1) * 8, :], [slot_tiles(wanted, vir, t) for t in range(tiles)])
        for t in range(tiles):
            turned = jnp.swapaxes(packed[t], 0, 1)
            for r in range(8):
                c = b * 8 + r
                out_ref[c // CK, c % CK, :, t * LANES : (t + 1) * LANES] = turned[r]


def pack_integrals(integrals, vir_irrep, tiles):
    width = tiles * LANES
    return pl.pallas_call(
        functools.partial(pack_integrals_kernel, tiles),
        out_shape=jax.ShapeDtypeStruct((YL, CK, AB, width), jnp.float32),
        grid=(AB // 16,),
        in_specs=[
            pl.BlockSpec(memory_space=pltpu.SMEM),
            pl.BlockSpec((16, CB, NV), lambda s: (s, 0, 0)),
        ],
        out_specs=pl.BlockSpec((YL, CK, 16, width), lambda s: (0, 0, s, 0)),
        compiler_params=pltpu.CompilerParams(vmem_limit_bytes=VMEM_LIMIT),
        cost_estimate=pl.CostEstimate(flops=10**6, bytes_accessed=3 * 10**6, transcendentals=0),
    )(vir_irrep, integrals)


def split(values):
    high = values.astype(jnp.bfloat16)
    return high, (values - high.astype(jnp.float32)).astype(jnp.bfloat16)


RING = [(0, 0, 0), (0, 1, 0)]
RING += [(1 + 2 * s + d, h, (s + 1) * (1 - 2 * d)) for s in range(3) for d in range(2) for h in range(YL)]
RING += [(7, 0, 4), (8, 0, 4)]


def contract_kernel(vir, labels_ref, t_ref, *refs):
    v_refs, (out_ref, v_high, v_low) = refs[:9], refs[9:]
    width = t_ref.shape[-1]

    @pl.when(pl.program_id(0) == 0)
    def _():
        for n, (array, part, _) in enumerate(RING):
            for k in range(CK):
                high, low = split(v_refs[array][part, k])
                v_high[n * AB : (n + 1) * AB, k * width : (k + 1) * width] = high
                v_low[n * AB : (n + 1) * AB, k * width : (k + 1) * width] = low

    total = jnp.zeros((Z * YL * AB, ROWS), jnp.float32)
    dims = (((1,), (1,)), ((), ()))
    for k in range(0, CK, 2):
        rows = jnp.concatenate([t_ref[0, :, k + n].reshape(ROWS, width) for n in range(2)], axis=1)
        high, low = split(rows)
        at = slice(k * width, (k + 2) * width)
        for left, right in ((v_high, high), (v_high, low), (v_low, high)):
            total += lax.dot_general(left[:, at], right, dims, preferred_element_type=jnp.float32)

    labels = labels_ref[0]
    z = lax.axis_index("z")
    for n, (_, part, behind) in enumerate(RING):
        source = YL * lax.rem(z - behind + Z, Z) + (n - len(RING) + YL if behind == 4 else part)
        for g in range(AB // 16):
            tb = (AB * lax.rem(source, Z * YL // SA) + 16 * g) // VT
            at = n * AB + 16 * g
            kept = jnp.where(labels == (vir[0] ^ vir[tb]), total[at : at + 16], 0.0)
            out_ref[0, source, 16 * g : 16 * (g + 1), :] = kept


def contract(received, ring, labels, vir_irrep):
    width = received.shape[-1]
    whole = pl.BlockSpec(memory_space=pltpu.VMEM)
    depth = CK * width
    return pl.pallas_call(
        contract_kernel,
        out_shape=jax.ShapeDtypeStruct((YL, JA, AB, ROWS), jnp.float32),
        grid=(YL,),
        in_specs=[
            pl.BlockSpec(memory_space=pltpu.SMEM),
            pl.BlockSpec((1, 1, ROWS), lambda s: (s, 0, 0)),
            pl.BlockSpec((1, JA, CK, PAIRS, width), lambda s: (s, 0, 0, 0, 0)),
        ]
        + [whole] * len(ring),
        out_specs=pl.BlockSpec((1, JA, AB, ROWS), lambda s: (s, 0, 0, 0)),
        scratch_shapes=[pltpu.VMEM((Z * YL * AB, depth), jnp.bfloat16)] * 2,
        compiler_params=pltpu.CompilerParams(vmem_limit_bytes=VMEM_LIMIT),
        cost_estimate=pl.CostEstimate(flops=6 * 768 * 512 * depth, bytes_accessed=10**7, transcendentals=0),
    )(vir_irrep, labels, received, *ring)


def ladder_parts(tiles, amplitudes, integrals, labels, occ_irrep, vir_irrep):
    forward = [(n, (n + 1) % Z) for n in range(Z)]
    backward = [(n, (n - 1) % Z) for n in range(Z)]
    own = lax.all_to_all(pack_integrals(integrals, vir_irrep, tiles), "yl", split_axis=0, concat_axis=0, tiled=True)
    ring = [own]
    ahead = behind = own
    for _ in range(3):
        behind = lax.ppermute(behind, "z", forward)
        ahead = lax.ppermute(ahead, "z", backward)
        ring += [behind, ahead]
    ring += [lax.ppermute(behind[:1], "z", forward), lax.ppermute(ahead[1:], "z", backward)]
    packed = pack_amplitudes(amplitudes, occ_irrep, vir_irrep, tiles)
    received = lax.all_to_all(
        packed.reshape((YL * JA,) + packed.shape[2:]), ("yl", "ja"), split_axis=0, concat_axis=0, tiled=True
    ).reshape(packed.shape)
    return contract(received, ring, labels, vir_irrep)


def reduce_kernel(parts_ref, out_ref):
    total = parts_ref[0]
    for n in range(1, YL * JA):
        total += parts_ref[n]
    padded = jnp.concatenate([total, jnp.zeros((LANES - AB, ROWS), jnp.float32)], axis=0)
    out_ref[...] = padded.T


def reduce_parts(parts):
    return pl.pallas_call(
        reduce_kernel,
        out_shape=jax.ShapeDtypeStruct((ROWS, LANES), jnp.float32),
        in_specs=[pl.BlockSpec(memory_space=pltpu.VMEM)],
        out_specs=pl.BlockSpec(memory_space=pltpu.VMEM),
        compiler_params=pltpu.CompilerParams(vmem_limit_bytes=VMEM_LIMIT),
    )(parts)


def local(amplitudes, integrals, occ_irrep, vir_irrep, occ_energy, vir_energy):
    z, yl, ja = lax.axis_index("z"), lax.axis_index("yl"), lax.axis_index("ja")
    occ_rows = lax.dynamic_slice_in_dim(occ_irrep, YL * NI * z, YL * NI).reshape(YL, 1, NI, 1)
    labels = jnp.bitwise_xor(occ_rows, occ_irrep.reshape(1, JA, 1, NI)).reshape(YL, 1, ROWS)
    largest = jnp.max(jnp.sum((vir_irrep[:, None] == vir_irrep[None, :]).astype(jnp.int32), axis=1))
    tier = jnp.where(largest <= 2, 0, jnp.where(largest <= 4, 1, 2))
    branches = [functools.partial(ladder_parts, tiles) for tiles in (1, 2, 3)]
    parts = lax.switch(tier, branches, amplitudes, integrals, labels, occ_irrep, vir_irrep)
    parts = lax.all_to_all(
        parts.reshape(YL * JA, AB, ROWS), ("yl", "ja"), split_axis=0, concat_axis=0, tiled=True
    )
    ladder = reduce_parts(parts).reshape(JA, PAIRS, LANES)
    mirror = lax.all_to_all(ladder, ("z", "yl"), split_axis=0, concat_axis=0, tiled=True)
    ladder = ladder.reshape(JA, NI, NI, LANES)[..., :AB].transpose(1, 0, 2, 3).reshape(NI, O, AB)
    mirror = mirror.reshape(JA, NI, NI, LANES)[..., :AB].transpose(2, 0, 1, 3).reshape(NI, O, AB)
    ab_energy = (vir_energy[:SA, None] + vir_energy[None, :]).reshape(SA * NV)
    ab_part = lax.dynamic_slice_in_dim(ab_energy, ja * AB, AB)
    occ_part = lax.dynamic_slice_in_dim(occ_energy, NI * (YL * z + yl), NI)
    denominator = occ_part[:, None, None] + occ_energy[None, :, None] - ab_part[None, None, :]
    return (ladder - mirror) / denominator


def solution(mesh):
    parts = Mesh(mesh.devices.reshape(Z, YL, JA), ("z", "yl", "ja"))
    rows = ("z", "yl")
    in_specs = (P(rows, "ja", None, None), P(rows, "ja", None), P(), P(), P(), P())
    return jax.shard_map(local, mesh=parts, in_specs=in_specs, out_specs=P(rows, None, "ja"), check_vma=False)
```

time: 902 us -> 155 us (0.17)
  waiting for transfers between devices: 720 us -> 73.6 us
  local copies, waits for them, and re-layouts: 65.5 us -> 7.97 us
  matrix products: 49.1 us -> 0 us
  other arithmetic: 34.2 us -> 2.77 us
  Pallas kernels: 0 us -> 27.4 us
  starting transfers between devices: 16.1 us -> 41.3 us
  between operations: 13.5 us -> 1.42 us
    all_gather x1 -> x0, waiting for transfers between devices: 468 us -> none  [local(): portion = lax.all_gather(integrals, 'ia', axis=0, tiled=True)]
    all_to_all x2 -> x4, waiting for transfers between devices: 176 us -> 31.7 us  [the longest x1 23.6 us: local(): lax.all_to_all(parts.reshape(YL * JA, AB, ROWS), ('yl', 'ja'), split_axis...]
    reduce_scatter x1 -> x0, waiting for transfers between devices: 75.5 us -> none  [local(): lax.psum_scatter(partial_value, 'ja', scatter_dimension=2, tiled=True)]
    dot_general x1 -> x0, matrix products: 49.1 us -> none  [contract_rows(): lax.dot_general(left_rows, right_rows, (((1,), (1,)), ((), ())), precisio...]
    ppermute x0 -> x8, waiting for transfers between devices: none -> 41.9 us  [the longest x3 38.1 us: ladder_parts(): behind = lax.ppermute(behind, 'z', forward)]
    select_n x2 -> x0, other arithmetic: 31.4 us -> none  [the longest x1 21.4 us: masked_rows(): return jnp.where(labels[:, None, None] == pair_cd[None], values, 0.0)]
    reshape x2 -> x0, local copies, waits for them, and re-layouts: 28.7 us -> none  [the longest x1 28.6 us: local(): masked_rows(portion, pair_ab, pair_cd)]
    pallas_call x0 -> x4, Pallas kernels: none -> 27.4 us  [the longest x1 13.2 us: pack_amplitudes(): pl.pallas_call(functools.partial(pack_amplitudes_kernel, tiles), out_shap...]
  transfers between devices with their start and end apart: 4 -> 12, of which waited for: 4 -> 6; matrix products, arithmetic and copies ran while one was open for 5% -> 1% of each run, Pallas kernels for 0% -> 9%
where the time goes in v1:
time: 155 us
  waiting for transfers between devices  73.6 us (47%)
  starting transfers between devices  41.3 us (27%)
  Pallas kernels  27.4 us (18%)
  local copies, waits for them, and re-layouts  7.97 us (5%)
  other arithmetic  2.77 us (2%)
    ppermute x3, waiting for transfers between devices, ladder_parts(): behind = lax.ppermute(behind, 'z', forward)  38.1 us
    all_to_all x1, waiting for transfers between devices, local(): lax.all_to_all(parts.reshape(YL * JA, AB, ROWS), ('yl', 'ja'), split_axis...  23.6 us
    pallas_call x1, Pallas kernels, pack_amplitudes(): pl.pallas_call(functools.partial(pack_amplitudes_kernel, tiles), out_shap...  13.2 us
    all_to_all x1, starting transfers between devices, local(): lax.all_to_all(parts.reshape(YL * JA, AB, ROWS), ('yl', 'ja'), split_axis...  9.99 us
    ppermute x3, starting transfers between devices, ladder_parts(): ahead = lax.ppermute(ahead, 'z', backward)  9.35 us
    all_to_all x1, starting transfers between devices, ladder_parts(): lax.all_to_all(packed.reshape((YL * JA,) + packed.shape[2:]), ('yl', 'ja'...  9.11 us
    pallas_call x1, Pallas kernels, contract(): pl.pallas_call(contract_kernel, out_shape=jax.ShapeDtypeStruct((YL, JA, A...  8.61 us
    all_to_all x1, waiting for transfers between devices, local(): lax.all_to_all(ladder, ('z', 'yl'), split_axis=0, concat_axis=0, tiled=True)  8.14 us
  transfers between devices with their start and end apart: 12, of which 6 were waited for; matrix products, arithmetic and copies ran while one was open for 1% of the time, Pallas kernels for 9%

profile of v1, /device:TPU:1, one launch (start us, length us, event | category | flops | bytes accessed | tf_op | source)
XLA Modules:
  0.0 154.7 jit_solution(2736825331820620453)
XLA Ops:
  0.0 0.9 convert_reduce_fusion
  0.9 0.6 reduce_max.9
  2.9 0.7 xor.33
  3.6 0.7 dynamic_slice.9
  4.8 96.9 %conditional.1 = (f32[2,16,48,256]{3,2,1,0:T(8,128)}) conditional(s32[]{:T(128)} %clamp.3, (f32[4,4,384,384]{3,2,1,0:T(8,128)}, s32[64]{0:T(128)}, s32[6]{0:T(128)}, f32[48,24,384]{2,1,0:T(8,128)}, s32[2,1,256]{2,0,1:T(2,128)S(1)}) %tuple.14, (f32[4,4,384,384]{3,2,1,0:T(8,128)}, s32[64]{0:T(128)}, s32[6]{0:T(128)}, ...), branch_computations={%region_2.3_spmd, %region_3.4_spmd, %region_4.5_spmd} | conditional | flops 10882635776 | bytes 166794144 | solution.py:235
  4.8 3.4 %branch_0_fun.4 = f32[2,12,48,128]{3,2,1,0:T(8,128)} custom-call(s32[6]{0:T(128)} %get-tuple-element.38.vir, f32[48,24,384]{2,1,0:T(8,128)} %get-tuple-element.43.v_ref), custom_call_target="tpu_custom_call" | custom-call | flops 1000000 | bytes 3000000 | tf_op jit(solution)/shard_map/cond/branch_0_fun/pallas_call | solution.py:115
  8.2 3.5 %all-to-all-start.1 = ((f32[2,12,48,128]{3,2,1,0:T(8,128)}), f32[2,12,48,128]{3,2,1,0:T(8,128)S(1)}, u32[]{:S(2)}, u32[]{:S(2)}) async-start(f32[2,12,48,128]{3,2,1,0:T(8,128)} %branch_0_fun.4), calls=%async_computation.1 | async-start | bytes 1179648 | tf_op jit(solution)/shard_map/cond/branch_0_fun/all_to_all | solution.py:195
  11.7 13.2 %branch_0_fun.3 = f32[2,16,12,16,128]{4,3,2,1,0:T(8,128)} custom-call(s32[64]{0:T(128)S(1)} %copy-done.14, s32[6]{0:T(128)S(1)} %copy-done.11, f32[16,384,384]{2,1,0:T(8,128)} %bitcast.23), custom_call_target="tpu_custom_call" | custom-call | flops 10000000 | bytes 14000000 | tf_op jit(solution)/shard_map/cond/branch_0_fun/pallas_call | solution.py:82
  24.9 0.8 copy-done.4
  25.7 9.1 %all-to-all-start = ((f32[32,12,16,128]{3,2,1,0:T(8,128)}), f32[32,12,16,128]{3,2,1,0:T(8,128)S(1)}, u32[]{:S(2)}, u32[]{:S(2)}) async-start(f32[32,12,16,128]{3,2,1,0:T(8,128)} %bitcast.28), calls=%async_computation | async-start | bytes 6291456 | tf_op jit(solution)/shard_map/cond/branch_0_fun/all_to_all | solution.py:204
  34.9 1.7 %collective-permute-start = (f32[2,12,48,128]{3,2,1,0:T(8,128)}, f32[2,12,48,128]{3,2,1,0:T(8,128)S(1)}, u32[]{:S(2)}, u32[]{:S(2)}) collective-permute-start(f32[2,12,48,128]{3,2,1,0:T(8,128)} %copy-done.4), channel_id=1, source_target_pairs={{0,32},{32,64},{64,96},{96,128},{128,160},{160,192},{192,224},{224... | collective-permute-start | bytes 1769480 | tf_op jit(solution)/shard_map/cond/branch_0_fun/ppermute | solution.py:199
  36.6 4.0 %collective-permute-start.1 = (f32[2,12,48,128]{3,2,1,0:T(8,128)}, f32[2,12,48,128]{3,2,1,0:T(8,128)S(1)}, u32[]{:S(2)}, u32[]{:S(2)}) collective-permute-start(f32[2,12,48,128]{3,2,1,0:T(8,128)} %copy-done.4), channel_id=1, source_target_pairs={{0,224},{32,0},{64,32},{96,64},{128,96},{160,128},{192,160},{224,1... | collective-permute-start | bytes 1769480 | tf_op jit(solution)/shard_map/cond/branch_0_fun/ppermute | solution.py:200
  40.6 13.7 %collective-permute-done.refs_1_ = f32[2,12,48,128]{3,2,1,0:T(8,128)S(1)} collective-permute-done((f32[2,12,48,128]{3,2,1,0:T(8,128)}, f32[2,12,48,128]{3,2,1,0:T(8,128)S(1)}, u32[]{:S(2)}, u32[]{:S(2)}) %collective-permute-start) | collective-permute-done | bytes 589856 | tf_op jit(solution)/shard_map/cond/branch_0_fun/ppermute | solution.py:199
  54.3 2.7 %collective-permute-start.3 = (f32[2,12,48,128]{3,2,1,0:T(8,128)S(1)}, f32[2,12,48,128]{3,2,1,0:T(8,128)S(1)}, u32[]{:S(2)}, u32[]{:S(2)}) collective-permute-start(f32[2,12,48,128]{3,2,1,0:T(8,128)S(1)} %collective-permute-done.1.refs_2_), channel_id=1, source_target_pairs={{0,224},{32,0},{64,32},{96,64},{128,96},{160,128},{192,160},{224,1... | collective-permute-start | bytes 1769480 | tf_op jit(solution)/shard_map/cond/branch_0_fun/ppermute | solution.py:200
  57.0 12.7 %collective-permute-done.2.refs_3_ = f32[2,12,48,128]{3,2,1,0:T(8,128)S(1)} collective-permute-done((f32[2,12,48,128]{3,2,1,0:T(8,128)S(1)}, f32[2,12,48,128]{3,2,1,0:T(8,128)S(1)}, u32[]{:S(2)}, u32[]{:S(2)}) %collective-permute-start.2) | collective-permute-done | bytes 589856 | tf_op jit(solution)/shard_map/cond/branch_0_fun/ppermute | solution.py:199
  69.7 2.7 %collective-permute-start.5 = (f32[2,12,48,128]{3,2,1,0:T(8,128)S(1)}, f32[2,12,48,128]{3,2,1,0:T(8,128)S(1)}, u32[]{:S(2)}, u32[]{:S(2)}) collective-permute-start(f32[2,12,48,128]{3,2,1,0:T(8,128)S(1)} %collective-permute-done.3.refs_4_), channel_id=1, source_target_pairs={{0,224},{32,0},{64,32},{96,64},{128,96},{160,128},{192,160},{224,1... | collective-permute-start | bytes 1769480 | tf_op jit(solution)/shard_map/cond/branch_0_fun/ppermute | solution.py:200
  72.3 11.7 %collective-permute-done.4.refs_5_ = f32[2,12,48,128]{3,2,1,0:T(8,128)S(1)} collective-permute-done((f32[2,12,48,128]{3,2,1,0:T(8,128)S(1)}, f32[2,12,48,128]{3,2,1,0:T(8,128)S(1)}, u32[]{:S(2)}, u32[]{:S(2)}) %collective-permute-start.4) | collective-permute-done | bytes 589856 | tf_op jit(solution)/shard_map/cond/branch_0_fun/ppermute | solution.py:199
  84.2 0.7 copy-done.9
  84.9 2.0 %collective-permute-start.7 = (f32[1,12,48,128]{3,2,1,0:T(8,128)S(1)}, f32[1,12,48,128]{3,2,1,0:T(8,128)}, u32[]{:S(2)}, u32[]{:S(2)}) collective-permute-start(f32[1,12,48,128]{3,2,1,0:T(8,128)S(1)} %slice.31), channel_id=1, source_target_pairs={{0,224},{32,0},{64,32},{96,64},{128,96},{160,128},{192,160},{224,1... | collective-permute-start | bytes 884744 | tf_op jit(solution)/shard_map/cond/branch_0_fun/ppermute | solution.py:202
  86.9 0.6 copy.28.labels_ref
  87.5 3.8 %collective-permute-done.6.refs_7_ = f32[1,12,48,128]{3,2,1,0:T(8,128)S(1)} collective-permute-done((f32[1,12,48,128]{3,2,1,0:T(8,128)S(1)}, f32[1,12,48,128]{3,2,1,0:T(8,128)S(1)}, u32[]{:S(2)}, u32[]{:S(2)}) %collective-permute-start.6) | collective-permute-done | bytes 294944 | tf_op jit(solution)/shard_map/cond/branch_0_fun/ppermute | solution.py:202
  91.4 0.7 copy-done.33
  92.1 1.0 copy-done.1
  93.1 8.6 %branch_0_fun.5 = f32[2,16,48,256]{3,2,1,0:T(8,128)} custom-call(s32[6]{0:T(128)S(1)} %copy-done.11, s32[2,1,256]{2,1,0:T(1,128)} %copy.28.labels_ref, f32[2,16,12,16,128]{4,3,2,1,0:T(8,128)} %bitcast.29, f32[2,12,48,128]{3,2,1,0:T(8,128)} %copy-done.4, f32[2,12,48,128]{3,2,1,0:T(8,128)} %copy-done.28, f32[2,12,48,128]{3,2,1,0:T(8,128)} %copy-done.29, ...), custom_call_target="tpu_custom_call" | custom-call | flops 3623878656 | bytes 10000000 | tf_op jit(solution)/shard_map/cond/branch_0_fun/pallas_call | solution.py:175
  101.7 10.0 %all-to-all-start.6 = ((f32[32,48,256]{2,1,0:T(8,128)}), f32[32,48,256]{2,1,0:T(8,128)S(1)}, u32[]{:S(2)}, u32[]{:S(2)}) async-start(f32[32,48,256]{2,1,0:T(8,128)} %bitcast.30), calls=%async_computation.6 | async-start | bytes 3145728 | tf_op jit(solution)/shard_map/all_to_all | solution.py:236
  111.7 23.6 %all-to-all-done.6.parts_ref = f32[32,48,256]{2,1,0:T(8,128)S(1)} async-done(((f32[32,48,256]{2,1,0:T(8,128)}), f32[32,48,256]{2,1,0:T(8,128)S(1)}, u32[]{:S(2)}, u32[]{:S(2)}) %all-to-all-start.6) | async-done | bytes 1572896 | tf_op jit(solution)/shard_map/all_to_all | solution.py:236
  135.3 1.2 copy-done
  136.5 2.2 %shard_map.64 = f32[256,128]{1,0:T(8,128)} custom-call(f32[32,48,256]{2,1,0:T(8,128)} %copy-done), custom_call_target="tpu_custom_call" | custom-call | tf_op jit(solution)/shard_map/pallas_call | solution.py:219
  138.7 5.5 %all-to-all-start.7 = ((f32[16,16,128]{2,1,0:T(8,128)}), f32[16,16,128]{2,1,0:T(8,128)S(1)}, u32[]{:S(2)}, u32[]{:S(2)}) async-start(f32[16,16,128]{2,1,0:T(8,128)} %bitcast.31), calls=%async_computation.7 | async-start | bytes 262144 | tf_op jit(solution)/shard_map/all_to_all | solution.py:240
  144.6 8.1 %all-to-all-done.7 = f32[16,16,128]{2,1,0:T(8,128)S(1)} async-done(((f32[16,16,128]{2,1,0:T(8,128)}), f32[16,16,128]{2,1,0:T(8,128)S(1)}, u32[]{:S(2)}, u32[]{:S(2)}) %all-to-all-start.7) | async-done | bytes 131104 | tf_op jit(solution)/shard_map/all_to_all | solution.py:240
  152.7 1.0 fusion
  153.9 0.7 copy.34
  (50 shorter events, 1.2 us)
Async XLA Ops:
  4.8 6.9 %copy-start.11 = (s32[6]{0:T(128)S(1)}, s32[6]{0:T(128)}, u32[]{:S(2)}) copy-start(s32[6]{0:T(128)} %get-tuple-element.38.vir) | copy-start | bytes 76 | tf_op jit(solution)/shard_map/cond
  4.8 6.9 %copy-start.14 = (s32[64]{0:T(128)S(1)}, s32[64]{0:T(128)}, u32[]{:S(2)}) copy-start(s32[64]{0:T(128)} %get-tuple-element.41.occ) | copy-start | bytes 772 | tf_op jit(solution)/shard_map/cond
  8.2 16.8 %all-to-all-start.1 = ((f32[2,12,48,128]{3,2,1,0:T(8,128)}), f32[2,12,48,128]{3,2,1,0:T(8,128)S(1)}, u32[]{:S(2)}, u32[]{:S(2)}) async-start(f32[2,12,48,128]{3,2,1,0:T(8,128)} %branch_0_fun.4), calls=%async_computation.1 | async-start | bytes 1179648 | tf_op jit(solution)/shard_map/cond/branch_0_fun/all_to_all | solution.py:195
  24.9 0.8 copy-start.4
  25.7 65.6 %all-to-all-start = ((f32[32,12,16,128]{3,2,1,0:T(8,128)}), f32[32,12,16,128]{3,2,1,0:T(8,128)S(1)}, u32[]{:S(2)}, u32[]{:S(2)}) async-start(f32[32,12,16,128]{3,2,1,0:T(8,128)} %bitcast.28), calls=%async_computation | async-start | bytes 6291456 | tf_op jit(solution)/shard_map/cond/branch_0_fun/all_to_all | solution.py:204
  34.9 19.4 %collective-permute-start = (f32[2,12,48,128]{3,2,1,0:T(8,128)}, f32[2,12,48,128]{3,2,1,0:T(8,128)S(1)}, u32[]{:S(2)}, u32[]{:S(2)}) collective-permute-start(f32[2,12,48,128]{3,2,1,0:T(8,128)} %copy-done.4), channel_id=1, source_target_pairs={{0,32},{32,64},{64,96},{96,128},{128,160},{160,192},{192,224},{224... | collective-permute-start | bytes 1769480 | tf_op jit(solution)/shard_map/cond/branch_0_fun/ppermute | solution.py:199
  36.6 17.7 %collective-permute-start.1 = (f32[2,12,48,128]{3,2,1,0:T(8,128)}, f32[2,12,48,128]{3,2,1,0:T(8,128)S(1)}, u32[]{:S(2)}, u32[]{:S(2)}) collective-permute-start(f32[2,12,48,128]{3,2,1,0:T(8,128)} %copy-done.4), channel_id=1, source_target_pairs={{0,224},{32,0},{64,32},{96,64},{128,96},{160,128},{192,160},{224,1... | collective-permute-start | bytes 1769480 | tf_op jit(solution)/shard_map/cond/branch_0_fun/ppermute | solution.py:200
  54.3 18.0 %copy-start.28 = (f32[2,12,48,128]{3,2,1,0:T(8,128)}, f32[2,12,48,128]{3,2,1,0:T(8,128)S(1)}, u32[]{:S(2)}) copy-start(f32[2,12,48,128]{3,2,1,0:T(8,128)S(1)} %collective-permute-done.refs_1_) | copy-start | bytes 1769476 | tf_op jit(solution)/shard_map/cond
  54.3 15.3 %collective-permute-start.2 = (f32[2,12,48,128]{3,2,1,0:T(8,128)S(1)}, f32[2,12,48,128]{3,2,1,0:T(8,128)S(1)}, u32[]{:S(2)}, u32[]{:S(2)}) collective-permute-start(f32[2,12,48,128]{3,2,1,0:T(8,128)S(1)} %collective-permute-done.refs_1_), channel_id=1, source_target_pairs={{0,32},{32,64},{64,96},{96,128},{128,160},{160,192},{192,224},{224... | collective-permute-start | bytes 1769480 | tf_op jit(solution)/shard_map/cond/branch_0_fun/ppermute | solution.py:199
  54.3 18.0 %copy-start.29 = (f32[2,12,48,128]{3,2,1,0:T(8,128)}, f32[2,12,48,128]{3,2,1,0:T(8,128)S(1)}, u32[]{:S(2)}) copy-start(f32[2,12,48,128]{3,2,1,0:T(8,128)S(1)} %collective-permute-done.1.refs_2_) | copy-start | bytes 1769476 | tf_op jit(solution)/shard_map/cond
  54.3 15.3 %collective-permute-start.3 = (f32[2,12,48,128]{3,2,1,0:T(8,128)S(1)}, f32[2,12,48,128]{3,2,1,0:T(8,128)S(1)}, u32[]{:S(2)}, u32[]{:S(2)}) collective-permute-start(f32[2,12,48,128]{3,2,1,0:T(8,128)S(1)} %collective-permute-done.1.refs_2_), channel_id=1, source_target_pairs={{0,224},{32,0},{64,32},{96,64},{128,96},{160,128},{192,160},{224,1... | collective-permute-start | bytes 1769480 | tf_op jit(solution)/shard_map/cond/branch_0_fun/ppermute | solution.py:200
  69.6 2.7 %copy-start.30 = (f32[2,12,48,128]{3,2,1,0:T(8,128)}, f32[2,12,48,128]{3,2,1,0:T(8,128)S(1)}, u32[]{:S(2)}) copy-start(f32[2,12,48,128]{3,2,1,0:T(8,128)S(1)} %collective-permute-done.2.refs_3_) | copy-start | bytes 1769476 | tf_op jit(solution)/shard_map/cond
  69.6 14.4 %collective-permute-start.4 = (f32[2,12,48,128]{3,2,1,0:T(8,128)S(1)}, f32[2,12,48,128]{3,2,1,0:T(8,128)S(1)}, u32[]{:S(2)}, u32[]{:S(2)}) collective-permute-start(f32[2,12,48,128]{3,2,1,0:T(8,128)S(1)} %collective-permute-done.2.refs_3_), channel_id=1, source_target_pairs={{0,32},{32,64},{64,96},{96,128},{128,160},{160,192},{192,224},{224... | collective-permute-start | bytes 1769480 | tf_op jit(solution)/shard_map/cond/branch_0_fun/ppermute | solution.py:199
  69.6 21.7 %copy-start.31 = (f32[2,12,48,128]{3,2,1,0:T(8,128)}, f32[2,12,48,128]{3,2,1,0:T(8,128)S(1)}, u32[]{:S(2)}) copy-start(f32[2,12,48,128]{3,2,1,0:T(8,128)S(1)} %collective-permute-done.3.refs_4_) | copy-start | bytes 1769476 | tf_op jit(solution)/shard_map/cond
  69.7 15.2 %collective-permute-start.5 = (f32[2,12,48,128]{3,2,1,0:T(8,128)S(1)}, f32[2,12,48,128]{3,2,1,0:T(8,128)S(1)}, u32[]{:S(2)}, u32[]{:S(2)}) collective-permute-start(f32[2,12,48,128]{3,2,1,0:T(8,128)S(1)} %collective-permute-done.3.refs_4_), channel_id=1, source_target_pairs={{0,224},{32,0},{64,32},{96,64},{128,96},{160,128},{192,160},{224,1... | collective-permute-start | bytes 1769480 | tf_op jit(solution)/shard_map/cond/branch_0_fun/ppermute | solution.py:200
  84.1 0.8 copy-start.9
  84.1 7.3 %collective-permute-start.6 = (f32[1,12,48,128]{3,2,1,0:T(8,128)S(1)}, f32[1,12,48,128]{3,2,1,0:T(8,128)S(1)}, u32[]{:S(2)}, u32[]{:S(2)}) collective-permute-start(f32[1,12,48,128]{3,2,1,0:T(8,128)S(1)} %slice.30), channel_id=1, source_target_pairs={{0,32},{32,64},{64,96},{96,128},{128,160},{160,192},{192,224},{224... | collective-permute-start | bytes 884744 | tf_op jit(solution)/shard_map/cond/branch_0_fun/ppermute | solution.py:202
  84.9 6.5 %copy-start.10 = (f32[2,12,48,128]{3,2,1,0:T(8,128)}, f32[2,12,48,128]{3,2,1,0:T(8,128)S(1)}, u32[]{:S(2)}) copy-start(f32[2,12,48,128]{3,2,1,0:T(8,128)S(1)} %collective-permute-done.5.refs_6_) | copy-start | bytes 1769476 | tf_op jit(solution)/shard_map/cond
  84.9 6.4 %collective-permute-start.7 = (f32[1,12,48,128]{3,2,1,0:T(8,128)S(1)}, f32[1,12,48,128]{3,2,1,0:T(8,128)}, u32[]{:S(2)}, u32[]{:S(2)}) collective-permute-start(f32[1,12,48,128]{3,2,1,0:T(8,128)S(1)} %slice.31), channel_id=1, source_target_pairs={{0,224},{32,0},{64,32},{96,64},{128,96},{160,128},{192,160},{224,1... | collective-permute-start | bytes 884744 | tf_op jit(solution)/shard_map/cond/branch_0_fun/ppermute | solution.py:202
  91.4 0.7 copy-start.33
  91.4 1.7 %copy-start.1 = (f32[32,12,16,128]{3,2,1,0:T(8,128)}, f32[32,12,16,128]{3,2,1,0:T(8,128)S(1)}, u32[]{:S(2)}) copy-start(f32[32,12,16,128]{3,2,1,0:T(8,128)S(1)} %all-to-all-done) | copy-start | bytes 9437188 | tf_op jit(solution)/shard_map/cond
  101.7 33.6 %all-to-all-start.6 = ((f32[32,48,256]{2,1,0:T(8,128)}), f32[32,48,256]{2,1,0:T(8,128)S(1)}, u32[]{:S(2)}, u32[]{:S(2)}) async-start(f32[32,48,256]{2,1,0:T(8,128)} %bitcast.30), calls=%async_computation.6 | async-start | bytes 3145728 | tf_op jit(solution)/shard_map/all_to_all | solution.py:236
  111.7 32.6 %copy-start.17 = (f32[384]{0:T(512)S(1)}, f32[384]{0:T(512)}, u32[]{:S(2)}) copy-start(f32[384]{0:T(512)} %param.14) | copy-start | bytes 4612
  111.7 32.6 %slice-start = ((f32[384]{0:T(512)}), f32[2]{0:T(128)S(1)}, s32[]{:S(2)}) async-start(f32[384]{0:T(512)} %param.14), calls=%async_computation.8 | async-start | bytes 1024 | tf_op jit(solution)/shard_map/slice | solution.py:243
  111.7 32.7 %copy-start.18 = (f32[64]{0:T(128)S(1)}, f32[64]{0:T(128)}, u32[]{:S(2)}) copy-start(f32[64]{0:T(128)} %param.13) | copy-start | bytes 772
  135.3 1.2 copy-start
  138.7 14.0 %all-to-all-start.7 = ((f32[16,16,128]{2,1,0:T(8,128)}), f32[16,16,128]{2,1,0:T(8,128)S(1)}, u32[]{:S(2)}, u32[]{:S(2)}) async-start(f32[16,16,128]{2,1,0:T(8,128)} %bitcast.31), calls=%async_computation.7 | async-start | bytes 262144 | tf_op jit(solution)/shard_map/all_to_all | solution.py:240
